TPU v7x, 128 devices: a whole 4x4x4 slice. The times are simulated.
128 devices in a mesh: ax: 16 (over z, y_lo, core), rad: 8 (over x, y_hi).
Axes of the slice: x: 4, y: 4 (y_hi: 2, y_lo: 2; y = y_hi * 2 + y_lo), z: 4, core: 2. Of those that a mesh axis runs over, the one named last changes fastest.
Arguments:
- velocity: float32 [3, 128, 512, 1024], P(None, 'ax', 'rad'), may hold values from -6 to 6
- viscosity: float32 [128, 512, 1024], P('ax', 'rad'), may hold values from 0.05 to 0.5
- inv_dx: float32 [128], P('ax'), may hold values from 0.5 to 2
- inv_dr: float32 [512], P('rad'), may hold values from 0.5 to 2
- inv_rt: float32 [512], P('rad'), may hold values from 0.5 to 2
- az_inverse: float32 [1024, 1024], replicated, may hold values from -0.5 to 2.5
- rad_inverse: float32 [512, 512], replicated, may hold values from -0.5 to 2.5
Outputs:
- velocity_next: float32 [3, 128, 512, 1024], P(None, 'ax', 'rad')
All inputs are finite; a program needn't handle non-finite values.
Results may differ from a plain program's by a relative error of at most 0.0003.
Values sent between devices are 32-bit elements; how exact they have to be, the bound alone decides.
No kernel may reach another device: no remote copies, remote signals or barrier semaphores. Data moves between devices by JAX's collectives and lax.ppermute only.
A program may use at most 256 MiB of HBM per device.

v0:
```python
import jax
import jax.numpy as jnp
from jax import lax
from jax.sharding import PartitionSpec as P

COEF = 0.25


def padded_2(block, sides, width):
    for axis, dim in sides:
        count = lax.axis_size(axis)
        forward = [(i, i + 1) for i in range(count - 1)]
        backward = [(target, source) for source, target in forward]
        low = lax.ppermute(
            lax.slice_in_dim(block, block.shape[dim] - width, None, axis=dim), axis, forward
        )
        high = lax.ppermute(lax.slice_in_dim(block, 0, width, axis=dim), axis, backward)
        block = jnp.concatenate([low, block, high], axis=dim)
    return block


def tendency(padded, inv_dx, inv_dr, inv_rt):
    planes = padded.shape[1] - 4
    radial = padded.shape[2] - 4

    def shifted(step_a, step_r):
        return padded[:, 2 + step_a : 2 + step_a + planes, 2 + step_r : 2 + step_r + radial, :]

    centre = shifted(0, 0)
    vel = centre[:3]
    visc = centre[3]
    metric_x = inv_dx[:, None, None]
    metric_r = inv_dr[None, :, None]
    metric_t = inv_rt[None, :, None]

    def parts(metric, plus_one, minus_one, plus_two, minus_two):
        deriv = (
            metric * (8.0 * (plus_one[:3] - minus_one[:3]) - (plus_two[:3] - minus_two[:3])) / 12.0
        )
        upper = 0.5 * (visc + plus_one[3]) * (plus_one[:3] - vel)
        lower = 0.5 * (visc + minus_one[3]) * (vel - minus_one[:3])
        return (deriv, metric * metric * (upper - lower))

    deriv_x, diff_x = parts(metric_x, shifted(1, 0), shifted(-1, 0), shifted(2, 0), shifted(-2, 0))
    deriv_r, diff_r = parts(metric_r, shifted(0, 1), shifted(0, -1), shifted(0, 2), shifted(0, -2))
    deriv_t, diff_t = parts(
        metric_t,
        jnp.roll(centre, -1, axis=3),
        jnp.roll(centre, 1, axis=3),
        jnp.roll(centre, -2, axis=3),
        jnp.roll(centre, 2, axis=3),
    )
    advect = vel[0] * deriv_x + vel[1] * deriv_t + vel[2] * deriv_r
    return vel + COEF * (diff_x + diff_t + diff_r - advect)


def local(velocity, viscosity, inv_dx, inv_dr, inv_rt, az_inverse, rad_inverse):
    fields = jnp.concatenate([velocity, viscosity[None]], axis=0)
    padded = padded_2(fields, (("ax", 1), ("rad", 2)), 2)
    rhs = tendency(padded, inv_dx, inv_dr, inv_rt)

    def radial(field):
        return jnp.einsum("rk,cakt->cart", rad_inverse, field, precision=lax.Precision.HIGHEST)

    solved = jnp.einsum("cars,ts->cart", rhs, az_inverse, precision=lax.Precision.HIGHEST)
    return lax.all_to_all(
        radial(lax.all_to_all(solved, "rad", split_axis=3, concat_axis=2, tiled=True)),
        "rad",
        split_axis=2,
        concat_axis=3,
        tiled=True,
    )


def solution(mesh):
    placed = (
        P(None, "ax", "rad", None),
        P("ax", "rad", None),
        P("ax"),
        P("rad"),
        P("rad"),
        P(),
        P(),
    )
    return jax.shard_map(
        local, mesh=mesh, in_specs=placed, out_specs=P(None, "ax", "rad", None), check_vma=False
    )
```

profile of v0, /device:TPU:96, one launch (start us, length us, event | category | flops | bytes accessed | tf_op | source)
XLA Modules:
  0.0 418.2 jit_solution(3006121644179621851)
XLA Ops:
  0.0 0.0 copy-start
  0.0 0.0 copy-start.7
  0.0 0.0 copy-start.1
  0.0 0.0 copy-start.2
  0.0 5.0 %fusion.75 = (f32[4,2,64,1024]{3,2,1,0:T(8,128)}, f32[4,2,64,1024]{3,2,1,0:T(8,128)}) fusion(f32[3,8,64,1024]{3,2,1,0:T(8,128)} %param.7, f32[1,8,64,1024]{3,2,1,0:T(8,128)} %bitcast.69), kind=kLoop, calls=%fused_computation.109 | loop fusion | flops 1048576 | bytes 12582912 | tf_op jit(solution)/shard_map/concatenate | solution.py:58
  5.1 2.9 collective-permute-start
  8.0 1.9 collective-permute-start.1
  9.9 0.0 copy-done.9
  9.9 0.0 copy-done.8
  9.9 0.6 mul.188
  10.5 0.0 copy-done.7
  10.5 0.6 mul.197
  11.1 0.0 copy-done.1
  11.1 0.0 copy-done.2
  11.1 0.4 fusion.89
  11.5 0.0 copy-start.6
  11.5 0.0 copy-start.5
  11.5 2.0 fusion.91
  13.5 5.1 %fusion.2 = f32[4,8,64,1022]{3,2,1,0:T(8,128)} fusion(f32[3,8,64,1024]{3,2,1,0:T(8,128)S(1)} %copy-done.1, f32[1,8,64,1024]{3,2,1,0:T(8,128)S(1)} %bitcast.72), kind=kLoop, calls=%fused_computation.22 | loop fusion | flops 2093056 | bytes 16760832 | tf_op jit(solution)/shard_map/concatenate | solution.py:58
  18.7 5.8 %fusion = (f32[4,8,64,1023]{3,2,1,0:T(8,128)S(1)}, f32[4,8,64,1023]{3,2,1,0:T(8,128)}) fusion(f32[3,8,64,1024]{3,2,1,0:T(8,128)S(1)} %copy-done.1, f32[1,8,64,1024]{3,2,1,0:T(8,128)S(1)} %bitcast.73), kind=kLoop, calls=%fused_computation.20 | loop fusion | flops 4190208 | bytes 25149440 | tf_op jit(solution)/shard_map/concatenate | solution.py:58
  24.4 0.0 copy-done.6
  24.4 2.1 fusion.83
  26.6 1.7 copy-done.3
  28.3 2.9 multiply_bitcast_fusion.2
  31.2 21.0 %collective-permute-done = f32[4,2,64,1024]{3,2,1,0:T(8,128)S(1)} collective-permute-done((f32[4,2,64,1024]{3,2,1,0:T(8,128)}, f32[4,2,64,1024]{3,2,1,0:T(8,128)S(1)}, u32[]{:S(2)}, u32[]{:S(2)}) %collective-permute-start) | collective-permute-done | bytes 2097184 | tf_op jit(solution)/shard_map/ppermute | solution.py:17
  52.1 3.2 collective-permute-done.1
  55.3 1.4 pad_maximum_fusion.32
  56.7 1.3 collective-permute-start.2
  58.0 0.0 slice-start
  58.0 0.0 slice-start.1
  58.0 7.1 %collective-permute-start.3 = (f32[4,12,2,1024]{3,2,1,0:T(2,128)S(1)}, f32[4,12,2,1024]{3,2,1,0:T(2,128)}, u32[]{:S(2)}, u32[]{:S(2)}) collective-permute-start(f32[4,12,2,1024]{3,2,1,0:T(2,128)S(1)} %get-tuple-element.10), channel_id=1, source_target_pairs={{0,1},{1,2},{2,3},{3,4},{4,5},{5,6},{6,7},{8,9},{9,10},{10,11},{11... | collective-permute-start | bytes 1179656 | tf_op jit(solution)/shard_map/ppermute | solution.py:14
  65.1 8.6 %pad_maximum_fusion = (f32[4,10,64,1024]{3,2,1,0:T(8,128)}, f32[4,10,64,1024]{3,2,1,0:T(8,128)}) fusion(f32[4,2,64,1024]{3,2,1,0:T(8,128)S(1)} %collective-permute-done, f32[1,8,64,1024]{3,2,1,0:T(8,128)S(1)} %bitcast.75, f32[3,8,64,1024]{3,2,1,0:T(8,128)S(1)} %copy-done.1, f32[4,2,64,1024]{3,2,1,0:T(8,128)} %collective-permute-done.1), kind=kLoop, calls=%fused_computation.18 | loop fusion | flops 10485760 | bytes 33554432 | tf_op jit(solution)/shard_map/concatenate | solution.py:18
  73.6 0.0 collective-permute-done.2
  73.6 4.8 %collective-permute-done.3 = f32[4,12,2,1024]{3,2,1,0:T(2,128)} collective-permute-done((f32[4,12,2,1024]{3,2,1,0:T(2,128)S(1)}, f32[4,12,2,1024]{3,2,1,0:T(2,128)}, u32[]{:S(2)}, u32[]{:S(2)}) %collective-permute-start.3) | collective-permute-done | bytes 393248 | tf_op jit(solution)/shard_map/ppermute | solution.py:14
  78.5 6.2 %fusion.79 = (f32[8,64,1024]{2,1,0:T(8,128)}, f32[8,64,1024]{2,1,0:T(8,128)}, f32[8,64,1024]{2,1,0:T(8,128)}, f32[8,64,1024]{2,1,0:T(8,128)}, f32[8,64,1024]{2,1,0:T(8,128)}) fusion(f32[8,64,1024]{2,1,0:T(8,128)S(1)} %copy-done.2, f32[4,12,2,1024]{3,2,1,0:T(2,128)S(1)} %collective-permute-done.2, f32[4,2,64,1024]{3,2,1,0:T(8,128)} %copy-done.4, ...), kind=kLoop, calls=%fused_computation.115 | loop fusion | flops 12058624 | bytes 34340864 | tf_op jit(solution)/shard_map/mul | solution.py:40
  84.6 68.5 %fusion.11 = f32[3,8,64,1024]{3,2,1,0:T(8,128)} fusion(f32[3,8,64,1024]{3,2,1,0:T(8,128)} %param.7, f32[4,12,2,1024]{3,2,1,0:T(2,128)} %collective-permute-done.3, f32[4,2,64,1024]{3,2,1,0:T(8,128)} %copy-done.4, f32[4,2,64,1024]{3,2,1,0:T(8,128)} %collective-permute-done.1, f32[1,8,64,1024]{3,2,1,0:T(8,128)S(1)} %bitcast.77, ...), kind=kOutput, calls=%fused_computation.32 | convolution fusion | flops 19428016128 | bytes 97257024 | tf_op jit(solution)/shard_map/cars,ts->cart/dot_general | solution.py:65
  153.1 9.8 %copy.22 = f32[3,8,64,1024]{2,1,0,3:T(8,128)} copy(f32[3,8,64,1024]{3,2,1,0:T(8,128)} %fusion.11) | data formatting | bytes 12582912 | tf_op jit(solution)/shard_map/cars,ts->cart/dot_general | solution.py:65
  162.9 12.6 %reshape.26 = f32[8,1,196608]{2,1,0:T(1,128)} reshape(f32[1024,3,8,64]{3,2,1,0:T(8,128)} %bitcast.78) | data formatting | bytes 12582912
  175.5 81.7 %all_to_all.36 = f32[8,1,196608]{2,1,0:T(1,128)} all-to-all(f32[8,1,196608]{2,1,0:T(1,128)} %reshape.26), channel_id=1, replica_groups=mesh['ax'=16,'rad'=8] {'rad'}, dimensions={0} | all-to-all | bytes 12582912 | tf_op jit(solution)/shard_map/all_to_all | solution.py:67
  257.2 0.6 broadcast.46
  257.8 19.5 %reduce = f32[8,196608]{1,0:T(8,128)} reduce(f32[8,1,196608]{2,1,0:T(1,128)} %all_to_all.36, f32[]{:T(128)} %broadcast.46), dimensions={1}, to_apply=%all_to_all.26.reduce_sub_computation | reduce | bytes 12582916 | tf_op jit(solution)/shard_map/all_to_all | solution.py:67
  277.4 12.2 %reshape.27 = f32[1024,3,8,64]{3,2,1,0:T(8,128)} reshape(f32[8,196608]{1,0:T(8,128)} %reduce) | data formatting | bytes 12582912
  289.6 9.8 %copy.24 = f32[3,8,8,64,128]{4,3,2,1,0:T(8,128)} copy(f32[3,8,8,64,128]{3,1,0,4,2:T(8,128)} %bitcast.79) | data formatting | bytes 12582912 | tf_op jit(solution)/shard_map/all_to_all | solution.py:67
  299.3 23.0 %convolution_bitcast_fusion = f32[3,8,512,128]{2,3,1,0:T(8,128)} fusion(f32[3,8,512,128]{3,2,1,0:T(8,128)} %bitcast.83, f32[512,512]{1,0:T(8,128)S(1)} %copy-done), kind=kOutput, calls=%fused_computation.107 | convolution fusion | flops 9663676416 | bytes 13631488 | tf_op jit(solution)/shard_map/rk,cakt->cart/dot_general | solution.py:63
  322.3 6.6 %copy.26 = f32[3,8,512,128]{3,1,0,2:T(8,128)} copy(f32[3,8,512,128]{2,3,1,0:T(8,128)} %convolution_bitcast_fusion) | data formatting | bytes 12582912 | tf_op jit(solution)/shard_map/rk,cakt->cart/transpose | solution.py:63
  328.8 76.0 %all_to_all.37 = f32[3,8,512,128]{3,1,0,2:T(8,128)S(1)} all-to-all(f32[3,8,512,128]{3,1,0,2:T(8,128)} %copy.26), channel_id=1, replica_groups=mesh['ax'=16,'rad'=8] {'rad'}, dimensions={2} | all-to-all | bytes 12582912 | tf_op jit(solution)/shard_map/all_to_all | solution.py:66
  404.9 6.3 %copy.28 = f32[3,8,64,8,128]{4,3,2,1,0:T(8,128)} copy(f32[3,8,64,8,128]{4,1,0,2,3:T(8,128)S(1)} %bitcast.82) | data formatting | bytes 12582912 | tf_op jit(solution)/shard_map/all_to_all | solution.py:66
  411.2 7.1 %all_to_all.33 = f32[3,8,64,1024]{3,2,1,0:T(8,128)} reshape(f32[3,8,64,8,128]{4,3,2,1,0:T(8,128)} %copy.28) | data formatting | bytes 12582912 | tf_op jit(solution)/shard_map/all_to_all | solution.py:66
  (11 shorter events, 0.0 us)
Async XLA Ops:
  0.0 299.3 %copy-start = (f32[512,512]{1,0:T(8,128)S(1)}, f32[512,512]{1,0:T(8,128)}, u32[]{:S(2)}) copy-start(f32[512,512]{1,0:T(8,128)} %param.13) | copy-start | bytes 3145732
  0.0 9.9 %copy-start.9 = (f32[8]{0:T(128)S(1)}, f32[8]{0:T(128)}, u32[]{:S(2)}) copy-start(f32[8]{0:T(128)} %param.9) | copy-start | bytes 100
  0.0 9.9 %copy-start.8 = (f32[64]{0:T(128)S(1)}, f32[64]{0:T(128)}, u32[]{:S(2)}) copy-start(f32[64]{0:T(128)} %param.11) | copy-start | bytes 772
  0.0 10.5 %copy-start.7 = (f32[64]{0:T(128)S(1)}, f32[64]{0:T(128)}, u32[]{:S(2)}) copy-start(f32[64]{0:T(128)} %param.10) | copy-start | bytes 772
  0.0 11.1 %copy-start.1 = (f32[3,8,64,1024]{3,2,1,0:T(8,128)S(1)}, f32[3,8,64,1024]{3,2,1,0:T(8,128)}, u32[]{:S(2)}) copy-start(f32[3,8,64,1024]{3,2,1,0:T(8,128)} %param.7) | copy-start | bytes 18874372
  0.0 11.1 %copy-start.2 = (f32[8,64,1024]{2,1,0:T(8,128)S(1)}, f32[8,64,1024]{2,1,0:T(8,128)}, u32[]{:S(2)}) copy-start(f32[8,64,1024]{2,1,0:T(8,128)} %param.8) | copy-start | bytes 6291460
  5.1 47.1 %collective-permute-start = (f32[4,2,64,1024]{3,2,1,0:T(8,128)}, f32[4,2,64,1024]{3,2,1,0:T(8,128)S(1)}, u32[]{:S(2)}, u32[]{:S(2)}) collective-permute-start(f32[4,2,64,1024]{3,2,1,0:T(8,128)} %get-tuple-element.20), channel_id=1, source_target_pairs={{8,0},{16,8},{24,16},{32,24},{40,32},{48,40},{56,48},{64,56},{72,6... | collective-permute-start | bytes 6291464 | tf_op jit(solution)/shard_map/ppermute | solution.py:17
  8.0 47.3 %collective-permute-start.1 = (f32[4,2,64,1024]{3,2,1,0:T(8,128)}, f32[4,2,64,1024]{3,2,1,0:T(8,128)}, u32[]{:S(2)}, u32[]{:S(2)}) collective-permute-start(f32[4,2,64,1024]{3,2,1,0:T(8,128)} %get-tuple-element.19), channel_id=1, source_target_pairs={{0,8},{8,16},{16,24},{24,32},{32,40},{40,48},{48,56},{56,64},{64,7... | collective-permute-start | bytes 6291464 | tf_op jit(solution)/shard_map/ppermute | solution.py:14
  11.5 12.9 %copy-start.6 = (f32[4,8,64,1]{3,2,1,0:T(8,128)}, f32[4,8,64,1]{3,2,1,0:T(8,128)S(1)}, u32[]{:S(2)}) copy-start(f32[4,8,64,1]{3,2,1,0:T(8,128)S(1)} %get-tuple-element.13) | copy-start | bytes 24580
  11.5 66.9 %copy-start.5 = (f32[4,8,64,1]{3,2,1,0:T(8,128)}, f32[4,8,64,1]{3,2,1,0:T(8,128)S(1)}, u32[]{:S(2)}) copy-start(f32[4,8,64,1]{3,2,1,0:T(8,128)S(1)} %get-tuple-element.14) | copy-start | bytes 24580
  24.4 3.9 copy-start.3
  52.1 13.0 %copy-start.4 = (f32[4,2,64,1024]{3,2,1,0:T(8,128)}, f32[4,2,64,1024]{3,2,1,0:T(8,128)S(1)}, u32[]{:S(2)}) copy-start(f32[4,2,64,1024]{3,2,1,0:T(8,128)S(1)} %collective-permute-done) | copy-start | bytes 6291460
  56.7 16.9 %collective-permute-start.2 = (f32[4,12,2,1024]{3,2,1,0:T(2,128)S(1)}, f32[4,12,2,1024]{3,2,1,0:T(2,128)S(1)}, u32[]{:S(2)}, u32[]{:S(2)}) collective-permute-start(f32[4,12,2,1024]{3,2,1,0:T(2,128)S(1)} %get-tuple-element.9), channel_id=1, source_target_pairs={{1,0},{2,1},{3,2},{4,3},{5,4},{6,5},{7,6},{9,8},{10,9},{11,10},{12... | collective-permute-start | bytes 1179656 | tf_op jit(solution)/shard_map/ppermute | solution.py:17
  58.0 20.5 %slice-start = ((s8[8388608]{0:T(1024)(128)(4,1)}), s8[4194304]{0:T(1024)(128)(4,1)S(1)}, s32[]{:S(2)}) async-start(s8[8388608]{0:T(1024)(128)(4,1)} %bitcast.80), calls=%async_computation.2 | async-start | bytes 8388608
  58.0 20.4 %slice-start.1 = ((s8[8388608]{0:T(1024)(128)(4,1)}), s8[4194304]{0:T(1024)(128)(4,1)S(1)}, s32[]{:S(2)}) async-start(s8[8388608]{0:T(1024)(128)(4,1)} %bitcast.80), calls=%async_computation.3 | async-start | bytes 8388608
  58.0 20.4 %collective-permute-start.3 = (f32[4,12,2,1024]{3,2,1,0:T(2,128)S(1)}, f32[4,12,2,1024]{3,2,1,0:T(2,128)}, u32[]{:S(2)}, u32[]{:S(2)}) collective-permute-start(f32[4,12,2,1024]{3,2,1,0:T(2,128)S(1)} %get-tuple-element.10), channel_id=1, source_target_pairs={{0,1},{1,2},{2,3},{3,4},{4,5},{5,6},{6,7},{8,9},{9,10},{10,11},{11... | collective-permute-start | bytes 1179656 | tf_op jit(solution)/shard_map/ppermute | solution.py:14
where the time goes:
time: 419 us; the launch traced here: 418 us
  blocking collectives  158 us (38%)
  matrix products  91.4 us (22%)
  local copies, waits for them, and re-layouts  66.6 us (16%)
  other arithmetic  60.2 us (14%)
  waiting for transfers between devices  28.9 us (7%)
  starting transfers between devices  13.2 us (3%)
    all_to_all x1, blocking collectives, local(): lax.all_to_all(solved, 'rad', split_axis=3, concat_axis=2, tiled=True)  81.7 us
    all_to_all x1, blocking collectives, local(): lax.all_to_all(radial(lax.all_to_all(solved, 'rad', split_axis=3, concat_...  76 us
    dot_general x1, matrix products, local(): jnp.einsum('cars,ts->cart', rhs, az_inverse, precision=lax.Precision.HIGH...  68.5 us
    unnamed x26, local copies, waits for them, and re-layouts  26.6 us
    dot_general x1, matrix products, radial(): jnp.einsum('rk,cakt->cart', rad_inverse, field, precision=lax.Precision.H...  23 us
    ppermute x2, waiting for transfers between devices, padded_2(): lax.ppermute(lax.slice_in_dim(block, 0, width, axis=dim), axis, backward)  21 us
    all_to_all x1, other arithmetic, local(): lax.all_to_all(solved, 'rad', split_axis=3, concat_axis=2, tiled=True)  19.5 us
    concatenate x5, other arithmetic, local(): fields = jnp.concatenate([velocity, viscosity[None]], axis=0)  18.3 us
  transfers between devices with their start and end apart: 4, of which 3 were waited for; matrix products, arithmetic and copies ran while one was open for 7% of the time, Pallas kernels for 0%

commit v1 on v0

--- a/solution.py
+++ b/solution.py
@@ -4,6 +4,13 @@
 from jax.sharding import PartitionSpec as P
 
 COEF = 0.25
+
+
+def stacked_exchange(value, name, split, join):
+    count = lax.axis_size(name)
+    blocks = jnp.stack(jnp.split(value, count, axis=split), axis=0)
+    blocks = lax.all_to_all(blocks, name, split_axis=0, concat_axis=0)
+    return jnp.concatenate(blocks, axis=join)
 
 
 def padded_2(block, sides, width):
@@ -64,7 +71,7 @@
 
     solved = jnp.einsum("cars,ts->cart", rhs, az_inverse, precision=lax.Precision.HIGHEST)
     return lax.all_to_all(
-        radial(lax.all_to_all(solved, "rad", split_axis=3, concat_axis=2, tiled=True)),
+        radial(stacked_exchange(solved, "rad", 3, 2)),
         "rad",
         split_axis=2,
         concat_axis=3,

time: 419 us -> 365 us (0.87); the launches traced: 418 us -> 358 us
  local copies, waits for them, and re-layouts: 66.6 us -> 32.4 us
  other arithmetic: 60.2 us -> 40 us
  waiting for transfers between devices: 28.9 us -> 24.3 us
    ppermute x2, waiting for transfers between devices: 21 us -> 1.1 us  [padded_2(): lax.ppermute(lax.slice_in_dim(block, 0, width, axis=dim), axis, backward)]
    all_to_all x1 -> x0, other arithmetic: 19.5 us -> none  [local(): lax.all_to_all(solved, 'rad', split_axis=3, concat_axis=2, tiled=True)]
    unnamed x26 -> x31, local copies, waits for them, and re-layouts: 26.6 us -> 10.2 us
    ppermute x2, waiting for transfers between devices: 7.97 us -> 23.2 us  [padded_2(): lax.ppermute(lax.slice_in_dim(block, block.shape[dim] - width, None, axis...]
    all_to_all x4 -> x2, local copies, waits for them, and re-layouts: 23.7 us -> 13.4 us  [local(): lax.all_to_all(radial(stacked_exchange(solved, 'rad', 3, 2)), 'rad', spli...]
    dot_general x1 -> x0, local copies, waits for them, and re-layouts: 9.76 us -> none  [local(): jnp.einsum('cars,ts->cart', rhs, az_inverse, precision=lax.Precision.HIGH...]
  transfers between devices with their start and end apart: 4 -> 4, of which waited for: 3 -> 3; matrix products, arithmetic and copies ran while one was open for 7% -> 8% of each run, Pallas kernels for 0% -> 0%
where the time goes in v1:
time: 365 us; the launch traced here: 358 us
  blocking collectives  155 us (42%)
  matrix products  91 us (25%)
  other arithmetic  40 us (11%)
  local copies, waits for them, and re-layouts  32.4 us (9%)
  waiting for transfers between devices  24.3 us (7%)
  starting transfers between devices  15 us (4%)
    all_to_all x1, blocking collectives, stacked_exchange(): blocks = lax.all_to_all(blocks, name, split_axis=0, concat_axis=0)  80.5 us
    all_to_all x1, blocking collectives, local(): lax.all_to_all(radial(stacked_exchange(solved, 'rad', 3, 2)), 'rad', spli...  74.9 us
    dot_general x1, matrix products, local(): jnp.einsum('cars,ts->cart', rhs, az_inverse, precision=lax.Precision.HIGH...  68.3 us
    ppermute x2, waiting for transfers between devices, padded_2(): lax.ppermute(lax.slice_in_dim(block, block.shape[dim] - width, None, axis...  23.2 us
    dot_general x1, matrix products, radial(): jnp.einsum('rk,cakt->cart', rad_inverse, field, precision=lax.Precision.H...  22.7 us
    concatenate x5, other arithmetic, local(): fields = jnp.concatenate([velocity, viscosity[None]], axis=0)  18 us
    all_to_all x2, local copies, waits for them, and re-layouts, local(): lax.all_to_all(radial(stacked_exchange(solved, 'rad', 3, 2)), 'rad', spli...  13.4 us
    unnamed x31, local copies, waits for them, and re-layouts  10.2 us
  transfers between devices with their start and end apart: 4, of which 3 were waited for; matrix products, arithmetic and copies ran while one was open for 8% of the time, Pallas kernels for 0%

profile of v1, /device:TPU:96, one launch (start us, length us, event | category | flops | bytes accessed | tf_op | source)
XLA Modules:
  0.0 358.2 jit_solution(12857092898732689098)
XLA Ops:
  0.0 0.0 copy-start
  0.0 0.0 copy-start.8
  0.0 0.0 copy-start.1
  0.0 0.0 copy-start.2
  0.0 5.0 %fusion.75 = (f32[4,2,64,1024]{3,2,1,0:T(8,128)}, f32[4,2,64,1024]{3,2,1,0:T(8,128)}) fusion(f32[3,8,64,1024]{3,2,1,0:T(8,128)} %param.7, f32[1,8,64,1024]{3,2,1,0:T(8,128)} %bitcast.96), kind=kLoop, calls=%fused_computation.109 | loop fusion | flops 1048576 | bytes 12582912 | tf_op jit(solution)/shard_map/concatenate | solution.py:65
  5.1 2.0 collective-permute-start.1
  7.1 4.5 %collective-permute-start = (f32[4,2,64,1024]{3,2,1,0:T(8,128)}, f32[4,2,64,1024]{3,2,1,0:T(8,128)}, u32[]{:S(2)}, u32[]{:S(2)}) collective-permute-start(f32[4,2,64,1024]{3,2,1,0:T(8,128)} %get-tuple-element.20), channel_id=1, source_target_pairs={{8,0},{16,8},{24,16},{32,24},{40,32},{48,40},{56,48},{64,56},{72,6... | collective-permute-start | bytes 6291464 | tf_op jit(solution)/shard_map/ppermute | solution.py:24
  11.7 0.0 copy-done.9
  11.7 0.0 copy-done.7
  11.7 0.6 mul.197
  12.3 0.0 copy-done.8
  12.3 0.5 mul.188
  12.8 1.7 fusion.91
  14.5 0.4 fusion.89
  15.0 5.2 %fusion.2 = f32[4,8,64,1022]{3,2,1,0:T(8,128)} fusion(f32[3,8,64,1024]{3,2,1,0:T(8,128)S(1)} %copy-done.1, f32[1,8,64,1024]{3,2,1,0:T(8,128)S(1)} %bitcast.99), kind=kLoop, calls=%fused_computation.22 | loop fusion | flops 2093056 | bytes 16760832 | tf_op jit(solution)/shard_map/concatenate | solution.py:65
  20.1 5.7 %fusion = (f32[4,8,64,1023]{3,2,1,0:T(8,128)S(1)}, f32[4,8,64,1023]{3,2,1,0:T(8,128)}) fusion(f32[3,8,64,1024]{3,2,1,0:T(8,128)S(1)} %copy-done.1, f32[1,8,64,1024]{3,2,1,0:T(8,128)S(1)} %bitcast.100), kind=kLoop, calls=%fused_computation.20 | loop fusion | flops 4190208 | bytes 25149440 | tf_op jit(solution)/shard_map/concatenate | solution.py:65
  25.8 2.1 fusion.83
  27.9 1.8 copy-done.3
  29.7 2.8 multiply_bitcast_fusion.2
  32.5 20.8 %collective-permute-done.1 = f32[4,2,64,1024]{3,2,1,0:T(8,128)S(1)} collective-permute-done((f32[4,2,64,1024]{3,2,1,0:T(8,128)}, f32[4,2,64,1024]{3,2,1,0:T(8,128)S(1)}, u32[]{:S(2)}, u32[]{:S(2)}) %collective-permute-start.1) | collective-permute-done | bytes 2097184 | tf_op jit(solution)/shard_map/ppermute | solution.py:21
  53.3 1.1 collective-permute-done
  54.4 1.4 pad_maximum_fusion.32
  55.8 1.3 collective-permute-start.2
  57.1 0.0 slice-start
  57.1 0.0 slice-start.1
  57.1 7.1 %collective-permute-start.3 = (f32[4,12,2,1024]{3,2,1,0:T(2,128)S(1)}, f32[4,12,2,1024]{3,2,1,0:T(2,128)}, u32[]{:S(2)}, u32[]{:S(2)}) collective-permute-start(f32[4,12,2,1024]{3,2,1,0:T(2,128)S(1)} %get-tuple-element.10), channel_id=1, source_target_pairs={{0,1},{1,2},{2,3},{3,4},{4,5},{5,6},{6,7},{8,9},{9,10},{10,11},{11... | collective-permute-start | bytes 1179656 | tf_op jit(solution)/shard_map/ppermute | solution.py:21
  64.2 0.0 copy-done.4
  64.2 8.5 %pad_maximum_fusion = (f32[4,10,64,1024]{3,2,1,0:T(8,128)}, f32[4,10,64,1024]{3,2,1,0:T(8,128)}) fusion(f32[4,2,64,1024]{3,2,1,0:T(8,128)} %collective-permute-done, f32[1,8,64,1024]{3,2,1,0:T(8,128)S(1)} %bitcast.102, f32[3,8,64,1024]{3,2,1,0:T(8,128)S(1)} %copy-done.1, f32[4,2,64,1024]{3,2,1,0:T(8,128)S(1)} %collective-permute-done.1), kind=kLoop, calls=%fused_computation.18 | loop fusion | flops 10485760 | bytes 33554432 | tf_op jit(solution)/shard_map/concatenate | solution.py:25
  72.7 0.0 collective-permute-done.2
  72.7 2.3 collective-permute-done.3
  75.1 0.0 slice-done
  75.1 6.1 %fusion.79 = (f32[8,64,1024]{2,1,0:T(8,128)}, f32[8,64,1024]{2,1,0:T(8,128)}, f32[8,64,1024]{2,1,0:T(8,128)}, f32[8,64,1024]{2,1,0:T(8,128)}, f32[8,64,1024]{2,1,0:T(8,128)}) fusion(f32[8,64,1024]{2,1,0:T(8,128)S(1)} %copy-done.2, f32[4,12,2,1024]{3,2,1,0:T(2,128)S(1)} %collective-permute-done.2, f32[4,2,64,1024]{3,2,1,0:T(8,128)} %collective-permute-done, ...), kind=kLoop, calls=%fused_computation.115 | loop fusion | flops 12058624 | bytes 34340864 | tf_op jit(solution)/shard_map/mul | solution.py:47
  81.2 68.3 %fusion.11 = f32[3,8,64,1024]{3,2,1,0:T(8,128)} fusion(f32[3,8,64,1024]{3,2,1,0:T(8,128)} %param.7, f32[4,12,2,1024]{3,2,1,0:T(2,128)} %collective-permute-done.3, f32[4,2,64,1024]{3,2,1,0:T(8,128)} %collective-permute-done, f32[4,2,64,1024]{3,2,1,0:T(8,128)} %copy-done.4, f32[1,8,64,1024]{3,2,1,0:T(8,128)S(1)} %bitcast.104, ...), kind=kOutput, calls=%fused_computation.32 | convolution fusion | flops 19428016128 | bytes 97257024 | tf_op jit(solution)/shard_map/cars,ts->cart/dot_general | solution.py:72
  149.5 1.2 fusion.100
  150.7 1.2 fusion.99
  151.9 1.2 fusion.98
  153.1 1.2 fusion.97
  154.3 1.2 fusion.96
  155.4 1.2 fusion.95
  156.6 1.2 fusion.94
  157.8 1.2 fusion.93
  159.0 80.5 %all_to_all.23 = f32[8,3,8,64,128]{4,3,2,1,0:T(8,128)S(1)} all-to-all(f32[8,3,8,64,128]{4,3,2,1,0:T(8,128)S(1)} %fusion.93), channel_id=1, replica_groups=mesh['ax'=16,'rad'=8] {'rad'}, dimensions={0} | all-to-all | bytes 12582912 | tf_op jit(solution)/shard_map/all_to_all | solution.py:12
  239.5 1.1 copy.16
  240.6 22.7 %convolution_bitcast_fusion = f32[3,8,512,128]{2,3,1,0:T(8,128)} fusion(f32[3,8,512,128]{3,2,1,0:T(8,128)S(1)} %bitcast.109, f32[512,512]{1,0:T(8,128)S(1)} %copy-done), kind=kOutput, calls=%fused_computation.107 | convolution fusion | flops 9663676416 | bytes 13631488 | tf_op jit(solution)/shard_map/rk,cakt->cart/dot_general | solution.py:70
  263.4 6.6 %copy.18 = f32[3,8,512,128]{3,1,0,2:T(8,128)} copy(f32[3,8,512,128]{2,3,1,0:T(8,128)} %convolution_bitcast_fusion) | data formatting | bytes 12582912 | tf_op jit(solution)/shard_map/rk,cakt->cart/transpose | solution.py:70
  270.0 74.9 %all_to_all.24 = f32[3,8,512,128]{3,1,0,2:T(8,128)S(1)} all-to-all(f32[3,8,512,128]{3,1,0,2:T(8,128)} %copy.18), channel_id=1, replica_groups=mesh['ax'=16,'rad'=8] {'rad'}, dimensions={2} | all-to-all | bytes 12582912 | tf_op jit(solution)/shard_map/all_to_all | solution.py:73
  344.9 6.3 %copy.20 = f32[3,8,64,8,128]{4,3,2,1,0:T(8,128)} copy(f32[3,8,64,8,128]{4,1,0,2,3:T(8,128)S(1)} %bitcast.108) | data formatting | bytes 12582912 | tf_op jit(solution)/shard_map/all_to_all | solution.py:73
  351.2 7.1 %all_to_all.20 = f32[3,8,64,1024]{3,2,1,0:T(8,128)} reshape(f32[3,8,64,8,128]{4,3,2,1,0:T(8,128)} %copy.20) | data formatting | bytes 12582912 | tf_op jit(solution)/shard_map/all_to_all | solution.py:73
  (14 shorter events, 0.0 us)
Async XLA Ops:
  0.0 240.6 %copy-start = (f32[512,512]{1,0:T(8,128)S(1)}, f32[512,512]{1,0:T(8,128)}, u32[]{:S(2)}) copy-start(f32[512,512]{1,0:T(8,128)} %param.13) | copy-start | bytes 3145732
  0.0 11.7 %copy-start.9 = (f32[8]{0:T(128)S(1)}, f32[8]{0:T(128)}, u32[]{:S(2)}) copy-start(f32[8]{0:T(128)} %param.9) | copy-start | bytes 100
  0.0 11.7 %copy-start.7 = (f32[64]{0:T(128)S(1)}, f32[64]{0:T(128)}, u32[]{:S(2)}) copy-start(f32[64]{0:T(128)} %param.10) | copy-start | bytes 772
  0.0 12.3 %copy-start.8 = (f32[64]{0:T(128)S(1)}, f32[64]{0:T(128)}, u32[]{:S(2)}) copy-start(f32[64]{0:T(128)} %param.11) | copy-start | bytes 772
  0.0 12.8 %copy-start.1 = (f32[3,8,64,1024]{3,2,1,0:T(8,128)S(1)}, f32[3,8,64,1024]{3,2,1,0:T(8,128)}, u32[]{:S(2)}) copy-start(f32[3,8,64,1024]{3,2,1,0:T(8,128)} %param.7) | copy-start | bytes 18874372
  0.0 12.8 %copy-start.2 = (f32[8,64,1024]{2,1,0:T(8,128)S(1)}, f32[8,64,1024]{2,1,0:T(8,128)}, u32[]{:S(2)}) copy-start(f32[8,64,1024]{2,1,0:T(8,128)} %param.8) | copy-start | bytes 6291460
  5.1 48.3 %collective-permute-start.1 = (f32[4,2,64,1024]{3,2,1,0:T(8,128)}, f32[4,2,64,1024]{3,2,1,0:T(8,128)S(1)}, u32[]{:S(2)}, u32[]{:S(2)}) collective-permute-start(f32[4,2,64,1024]{3,2,1,0:T(8,128)} %get-tuple-element.19), channel_id=1, source_target_pairs={{0,8},{8,16},{16,24},{24,32},{32,40},{40,48},{48,56},{56,64},{64,7... | collective-permute-start | bytes 6291464 | tf_op jit(solution)/shard_map/ppermute | solution.py:21
  7.1 47.3 %collective-permute-start = (f32[4,2,64,1024]{3,2,1,0:T(8,128)}, f32[4,2,64,1024]{3,2,1,0:T(8,128)}, u32[]{:S(2)}, u32[]{:S(2)}) collective-permute-start(f32[4,2,64,1024]{3,2,1,0:T(8,128)} %get-tuple-element.20), channel_id=1, source_target_pairs={{8,0},{16,8},{24,16},{32,24},{40,32},{48,40},{56,48},{64,56},{72,6... | collective-permute-start | bytes 6291464 | tf_op jit(solution)/shard_map/ppermute | solution.py:24
  14.9 10.9 %copy-start.6 = (f32[4,8,64,1]{3,2,1,0:T(8,128)}, f32[4,8,64,1]{3,2,1,0:T(8,128)S(1)}, u32[]{:S(2)}) copy-start(f32[4,8,64,1]{3,2,1,0:T(8,128)S(1)} %get-tuple-element.13) | copy-start | bytes 24580
  14.9 60.1 %copy-start.5 = (f32[4,8,64,1]{3,2,1,0:T(8,128)}, f32[4,8,64,1]{3,2,1,0:T(8,128)S(1)}, u32[]{:S(2)}) copy-start(f32[4,8,64,1]{3,2,1,0:T(8,128)S(1)} %get-tuple-element.14) | copy-start | bytes 24580
  25.8 3.9 %copy-start.3 = (f32[4,8,64,1023]{3,2,1,0:T(8,128)}, f32[4,8,64,1023]{3,2,1,0:T(8,128)S(1)}, u32[]{:S(2)}) copy-start(f32[4,8,64,1023]{3,2,1,0:T(8,128)S(1)} %get-tuple-element.11) | copy-start | bytes 25141252
  53.3 10.9 %copy-start.4 = (f32[4,2,64,1024]{3,2,1,0:T(8,128)}, f32[4,2,64,1024]{3,2,1,0:T(8,128)S(1)}, u32[]{:S(2)}) copy-start(f32[4,2,64,1024]{3,2,1,0:T(8,128)S(1)} %collective-permute-done.1) | copy-start | bytes 6291460
  55.8 16.9 %collective-permute-start.2 = (f32[4,12,2,1024]{3,2,1,0:T(2,128)S(1)}, f32[4,12,2,1024]{3,2,1,0:T(2,128)S(1)}, u32[]{:S(2)}, u32[]{:S(2)}) collective-permute-start(f32[4,12,2,1024]{3,2,1,0:T(2,128)S(1)} %get-tuple-element.9), channel_id=1, source_target_pairs={{1,0},{2,1},{3,2},{4,3},{5,4},{6,5},{7,6},{9,8},{10,9},{11,10},{12... | collective-permute-start | bytes 1179656 | tf_op jit(solution)/shard_map/ppermute | solution.py:24
  57.1 17.9 %slice-start = ((s8[8388608]{0:T(1024)(128)(4,1)}), s8[4194304]{0:T(1024)(128)(4,1)S(1)}, s32[]{:S(2)}) async-start(s8[8388608]{0:T(1024)(128)(4,1)} %bitcast.105), calls=%async_computation.2 | async-start | bytes 8388608
  57.1 17.9 %slice-start.1 = ((s8[8388608]{0:T(1024)(128)(4,1)}), s8[4194304]{0:T(1024)(128)(4,1)S(1)}, s32[]{:S(2)}) async-start(s8[8388608]{0:T(1024)(128)(4,1)} %bitcast.105), calls=%async_computation.3 | async-start | bytes 8388608
  57.1 17.9 %collective-permute-start.3 = (f32[4,12,2,1024]{3,2,1,0:T(2,128)S(1)}, f32[4,12,2,1024]{3,2,1,0:T(2,128)}, u32[]{:S(2)}, u32[]{:S(2)}) collective-permute-start(f32[4,12,2,1024]{3,2,1,0:T(2,128)S(1)} %get-tuple-element.10), channel_id=1, source_target_pairs={{0,1},{1,2},{2,3},{3,4},{4,5},{5,6},{6,7},{8,9},{9,10},{10,11},{11... | collective-permute-start | bytes 1179656 | tf_op jit(solution)/shard_map/ppermute | solution.py:21
